TPU v7x, 32 devices: a whole 2x2x4 slice. The times are simulated.
32 devices in a mesh: groups: 2 (over y), tile: 16 (over z, x, core).
Axes of the slice: x: 2, y: 2, z: 4, core: 2. Of those that a mesh axis runs over, the one named last changes fastest.
Arguments:
- object_slices: float32 [4096, 2, 2, 256], P(('groups', 'tile')), parts along dimension 0, may hold values from -4 to 4
- probe_field: float32 [256, 2, 2, 128], P(('groups', 'tile')), parts along dimension 0, may hold values from -2.5 to 2.5
- patterns: float32 [512, 128, 128], P(('groups', 'tile')), parts along dimension 0, may hold values from 0 to 2
- row_offsets: int32 [512], P(('groups', 'tile')), parts along dimension 0, may hold values from 0 to 127
- col_offsets: int32 [512], P(('groups', 'tile')), parts along dimension 0, may hold values from 0 to 128
- counts: int32 [32], P(('groups', 'tile')), parts along dimension 0, may hold values from 1 to 16, as said below
Outputs:
- object_grad: float32 [4096, 2, 2, 256], P(('groups', 'tile')), parts along dimension 0
- probe_grad: float32 [256, 2, 2, 128], P(('groups', 'tile')), parts along dimension 0
There are 2 independent parts, one for each index of `groups`. A program takes and returns all parts, laid end to end along the dimension named above; each array names one. Nothing has to cross between parts.
Inputs may be any that keep to these rules, and one draw needn't show every extreme that they name: `counts`: each tile has 1 to 16 live slots, and one tile of every draw has 16.
All inputs are finite; a program needn't handle non-finite values.
Results may differ from a plain program's by a relative error of at most 0.0003.
Values sent between devices are 32-bit elements; how exact they have to be, the bound alone decides.
No kernel may reach another device: no remote copies, remote signals or barrier semaphores. Data moves between devices by JAX's collectives and lax.ppermute only.
A program may use at most 64 MiB of HBM per device.

v0:
```python
import functools
import math

import jax
import jax.numpy as jnp
import numpy as np
from jax import lax
from jax.experimental import pallas as pl
from jax.experimental.pallas import tpu as pltpu
from jax.sharding import PartitionSpec as P

GROUP_DEV = 16
KAPPA = 4.0
MODES = 2
SLICES = 2
HALVES = 2
AHEAD = (0, 8, 4, 12, 2, 10, 6, 14)
BACK = (0, 2, 8, 10, 4, 6, 12, 14)


def factors(extent):
    counter = np.arange(extent)
    half = extent // 2
    dft = np.exp(-2j * np.pi * (counter[:, None] * counter[None, :] % extent) / extent) / math.sqrt(extent)
    freq = ((counter + extent // 2) % extent - extent // 2) / extent
    prop = np.conj(dft) @ (np.exp(-1j * np.pi * KAPPA * freq**2)[:, None] * dft)
    whole = [part for matrix in (dft, prop) for part in (matrix.real, matrix.imag)]
    same, cross = prop[:half, :half], prop[:half, half:]
    even, odd = dft[0::2, :half], dft[1::2, :half]
    halves = [even, odd, np.conj(even.T), np.conj(odd.T),
              (same + cross) / 2, (same - cross) / 2, np.conj(same + cross) / 2, np.conj(same - cross) / 2]
    halves = [np.block([[m.real, -m.imag], [m.imag, m.real]]) for m in halves]
    return np.stack(whole + halves).astype(np.float32)


def split(value):
    high = value.astype(jnp.bfloat16)
    low = (value - high.astype(jnp.float32)).astype(jnp.bfloat16)
    return high, low


def prepare(own_ref, patterns_ref, factors_ref, planes_out, patterns_out, mats_out, half_out, own, parts, sems):
    copies = [pltpu.make_async_copy(source, target, sems.at[i]) for i, (source, target) in enumerate(
        ((factors_ref, parts), (own_ref, own), (patterns_ref, patterns_out)))]
    for copy in copies:
        copy.start()
    copies[0].wait()
    extent = parts.shape[1]
    for kind in range(2):
        real, imag = split(parts[2 * kind]), split(parts[2 * kind + 1])
        for conj in range(2):
            for k in range(2):
                mat = 4 * kind + 2 * conj + k
                upper, lower = (-imag[k], imag[k]) if conj else (imag[k], -imag[k])
                mats_out[mat, :extent, :extent] = real[k]
                mats_out[mat, :extent, extent:] = upper
                mats_out[mat, extent:, :extent] = lower
                mats_out[mat, extent:, extent:] = real[k]
    for k in range(half_out.shape[0]):
        high, low = split(parts[4 + k])
        half_out[k, :extent, :extent] = high
        half_out[k, :extent, extent:] = high
        half_out[k, extent:, :extent] = low
        half_out[k, extent:, extent:] = low
    copies[1].wait()
    rows = planes_out.shape[1]
    for layer in range(SLICES):
        for half in range(HALVES):
            for part in range(2):
                source = (layer * HALVES + half) * 2 + part
                plane = (layer * 2 + part) * HALVES + half
                planes_out[plane] = own[pl.ds(source, rows, stride=8), :]
    copies[2].wait()


def times(a, b):
    return [a[0] * b[0] - a[1] * b[1], a[0] * b[1] + a[1] * b[0]]


def conj_times(a, b):
    return [a[0] * b[0] + a[1] * b[1], a[0] * b[1] - a[1] * b[0]]


def add(a, b):
    return [a[0] + b[0], a[1] + b[1]]


def member_rows(member, order, share):
    return pl.ds(pl.multiple_of(lax.bitwise_xor(member, order) * share, share), share)


def place(probe_ref, keep_out, send_out):
    lanes, extent = probe_ref.shape[:2]
    share = extent // GROUP_DEV
    member = lax.rem(lax.axis_index("tile"), GROUP_DEV)
    for odd, ref in enumerate((keep_out, send_out)):
        for block, order in enumerate(BACK):
            for k in range(lanes):
                rows = pl.ds(block * share * lanes + k, share, stride=lanes)
                ref[rows, :] = probe_ref[k, member_rows(member, order + odd, share), :]


def kernel(call, scalars_ref, patterns_ref, mats_ref, half_ref, *refs):
    most, extent = patterns_ref.shape[:2]
    middle = extent // 2
    tile_rows = extent
    lanes = 2 * MODES
    modes = range(MODES)
    if call == 0:
        own_ref, low_ref, near_ref, far_ref, obj, acc, probe, probe_acc = refs
    elif call == 1:
        high_ref, old_obj, old_acc, probe, old_probe_acc, obj, acc, probe_acc, high_out = refs
    else:
        obj, old_acc, probe, old_probe_acc, own_out, low_out, probe_acc, acc = refs

    def pieces():
        for layer in range(SLICES):
            for half in range(HALVES):
                for part in range(2):
                    yield (layer * 2 + part) * HALVES + half, (layer * HALVES + half) * 2 + part

    if call == 0:
        share = extent // GROUP_DEV
        member = lax.rem(lax.axis_index("tile"), GROUP_DEV)
        for plane, source in pieces():
            obj[plane, :tile_rows] = own_ref[plane]
            obj[plane, tile_rows:tile_rows + middle] = low_ref[pl.ds(source, middle, stride=8), :]
            obj[plane, tile_rows + middle:] = jnp.zeros((extent - middle, extent), jnp.float32)
        for odd, ref in enumerate((near_ref, far_ref)):
            for block, order in enumerate(AHEAD):
                for k in range(lanes):
                    rows = pl.ds(block * share * lanes + k, share, stride=lanes)
                    probe[k, member_rows(member, order + odd, share), :] = ref[rows, :]
        acc[...] = jnp.zeros(acc.shape, jnp.float32)
        probe_acc[...] = jnp.zeros(probe_acc.shape, jnp.float32)
    else:
        if call == 1:
            for plane, source in pieces():
                obj[plane, :tile_rows + middle] = old_obj[plane, :tile_rows + middle]
                obj[plane, tile_rows + middle:] = high_ref[pl.ds(source, extent - middle, stride=8), :]
        acc[...] = old_acc[...]
        probe_acc[...] = old_probe_acc[...]

    def right(fields, kind, conj):
        high_m, low_m = mats_ref[4 * kind + 2 * conj], mats_ref[4 * kind + 2 * conj + 1]
        rows = jnp.concatenate([jnp.concatenate(f[m], axis=1) for f in fields for m in modes], axis=0)
        high, low = split(rows)
        out = jnp.dot(jnp.concatenate([high, low, high], axis=1), jnp.concatenate([high_m, high_m, low_m], axis=0),
                      preferred_element_type=jnp.float32)
        return [[[out[(i * MODES + m) * extent:(i * MODES + m + 1) * extent, c * extent:(c + 1) * extent]
                  for c in range(2)] for m in modes] for i in range(len(fields))]

    def left(fields, kind, conj):
        middle = extent // 2
        cols = [jnp.concatenate([f[m][c] for f in fields for m in modes], axis=1) for c in range(2)]
        upper, lower = [c[:middle] for c in cols], [c[middle:] for c in cols]
        if kind == 1 or not conj:
            upper, lower = add(upper, lower), [u - v for u, v in zip(upper, lower)]
        halves = []
        for k, pieces in enumerate((upper, lower)):
            high, low = split(jnp.concatenate(pieces, axis=0))
            out = jnp.dot(half_ref[4 * kind + 2 * conj + k], jnp.concatenate([high, low], axis=0),
                          preferred_element_type=jnp.float32)
            out = out[:extent] + out[extent:]
            halves.append([out[:middle], out[middle:]])
        upper, lower = halves
        if kind == 1 or conj:
            upper, lower = add(upper, lower), [u - v for u, v in zip(upper, lower)]
        out = [jnp.concatenate([upper[c], lower[c]], axis=0) for c in range(2)]
        return [[[out[c][:, (i * MODES + m) * extent:(i * MODES + m + 1) * extent] for c in range(2)]
                 for m in modes] for i in range(len(fields))]

    lane = lax.broadcasted_iota(jnp.int32, (extent, extent), 1)

    low_count = scalars_ref[3 * most]
    ending = lax.shift_right_logical(low_count, 3) * 4
    beginning = lax.shift_right_logical(low_count - ending, 2) * 4
    first = (0, beginning + ending, beginning)[call]
    count = (beginning, scalars_ref[3 * most + 1] - beginning - ending, ending)[call]

    def numbered(slot):
        return scalars_ref[2 * most + jnp.minimum(first + slot, most - 1)]

    def corner(slot):
        return scalars_ref[numbered(slot)], scalars_ref[most + numbered(slot)]

    def window(slot):
        r, c = corner(slot)
        shift = lax.rem(extent - c, extent)
        layers = []
        for layer in range(SLICES):
            parts = []
            for part in range(2):
                plane = (layer * 2 + part) * HALVES
                joined = jnp.where(lane >= c, obj[plane, pl.ds(r, extent), :], obj[plane + 1, pl.ds(r, extent), :])
                parts.append(pltpu.roll(joined, shift, 1))
            layers.append(parts)
        return layers

    def deposit(slot, layer, grad):
        r, c = corner(slot)
        for part in range(2):
            plane = (layer * 2 + part) * HALVES
            rolled = pltpu.roll(grad[part], lax.rem(c, extent), 1)
            acc[plane, pl.ds(r, extent), :] += jnp.where(lane >= c, rolled, 0.0)
            acc[plane + 1, pl.ds(r, extent), :] += jnp.where(lane >= c, 0.0, rolled)

    def measured(slot):
        return jnp.concatenate([patterns_ref[numbered(slot), pl.ds(k, extent // 2, stride=2), :] for k in range(2)], axis=0)

    def steps(slots):
        n = range(len(slots))
        field = [[probe[2 * m], probe[2 * m + 1]] for m in modes]
        objects = [window(slot) for slot in slots]
        state = right([[times(field[m], objects[i][0]) for m in modes] for i in n], 1, 0)
        yield
        entering = left(state, 1, 0)
        yield
        state = right([[times(entering[i][m], objects[i][1]) for m in modes] for i in n], 0, 0)
        yield
        state = left(state, 0, 0)
        yield
        weight = []
        for i in n:
            intensity = sum(state[i][m][c] * state[i][m][c] for m in modes for c in range(2))
            weight.append(jnp.where(slots[i] < count, 2.0 * (intensity - measured(slots[i])), 0.0))
        state = right([[[weight[i] * state[i][m][c] for c in range(2)] for m in modes] for i in n], 0, 1)
        yield
        state = left(state, 0, 1)
        yield
        for i in n:
            grad = conj_times(entering[i][0], state[i][0])
            for m in modes[1:]:
                grad = add(grad, conj_times(entering[i][m], state[i][m]))
            deposit(slots[i], 1, grad)
        state = right([[conj_times(objects[i][1], state[i][m]) for m in modes] for i in n], 1, 1)
        yield
        state = left(state, 1, 1)
        yield
        for i in n:
            grad = conj_times(field[0], state[i][0])
            for m in modes[1:]:
                grad = add(grad, conj_times(field[m], state[i][m]))
            deposit(slots[i], 0, grad)
        for m in modes:
            term = conj_times(objects[0][0], state[0][m])
            for i in n[1:]:
                term = add(term, conj_times(objects[i][0], state[i][m]))
            probe_acc[2 * m] += term[0]
            probe_acc[2 * m + 1] += term[1]

    def run(*sets):
        running = [steps(slots) for slots in sets]
        while running:
            running = [r for r in running if next(r, "done") is None]

    fours = lax.shift_right_logical(count + 1, 2)
    left_over = count - 4 * fours

    def four(j, carry):
        run([4 * j, 4 * j + 1], [4 * j + 2, 4 * j + 3])
        return carry

    lax.fori_loop(0, fours, four, 0)

    if call == 1:
        @pl.when(left_over == 2)
        def _():
            run([4 * fours], [4 * fours + 1])

        @pl.when(left_over == 1)
        def _():
            run([4 * fours])

        for plane, target in pieces():
            high_out[pl.ds(target, extent - middle, stride=8), :] = acc[plane, tile_rows + middle:]
    elif call == 2:
        for plane, target in pieces():
            own_out[pl.ds(target, tile_rows, stride=8), :] = acc[plane, :tile_rows]
            low_out[pl.ds(target, middle, stride=8), :] = acc[plane, tile_rows:tile_rows + middle]


def prepared(own, patterns):
    extent = patterns.shape[1]
    vmem = pl.BlockSpec(memory_space=pltpu.VMEM)
    parts = jnp.asarray(factors(extent))
    return pl.pallas_call(
        prepare,
        out_shape=(
            jax.ShapeDtypeStruct((8, own.shape[0] // 8, own.shape[1]), jnp.float32),
            jax.ShapeDtypeStruct(patterns.shape, jnp.float32),
            jax.ShapeDtypeStruct((8, 2 * extent, 2 * extent), jnp.bfloat16),
            jax.ShapeDtypeStruct((8, 2 * extent, 2 * extent), jnp.bfloat16),
        ),
        in_specs=[pl.BlockSpec(memory_space=pltpu.HBM)] * 3,
        out_specs=(vmem,) * 4,
        scratch_shapes=[
            pltpu.VMEM(own.shape, jnp.float32),
            pltpu.VMEM(parts.shape, jnp.float32),
            pltpu.SemaphoreType.DMA((3,)),
        ],
        compiler_params=pltpu.CompilerParams(vmem_limit_bytes=16 * 1024 * 1024),
        cost_estimate=pl.CostEstimate(flops=0, bytes_accessed=6 * 1024 * 1024, transcendentals=0),
    )(own, patterns, parts)


def terms(call, scalars, patterns, mats, *operands):
    extent = patterns.shape[1]
    smem = pl.BlockSpec(memory_space=pltpu.SMEM)
    vmem = pl.BlockSpec(memory_space=pltpu.VMEM)
    rows = pltpu.VMEM((8, 2 * extent, extent), jnp.float32)
    planes = jax.ShapeDtypeStruct((8, 2 * extent, extent), jnp.float32)
    probe = jax.ShapeDtypeStruct((2 * MODES, extent, extent), jnp.float32)
    whole = jax.ShapeDtypeStruct((8 * extent, extent), jnp.float32)
    half = jax.ShapeDtypeStruct((4 * extent, extent), jnp.float32)
    outs = ((planes, planes, probe, probe), (planes, planes, probe, half), (whole, half, probe))[call]
    operands = (scalars, patterns, *mats, *operands)
    return pl.pallas_call(
        functools.partial(kernel, call),
        out_shape=outs,
        in_specs=[smem] + [vmem] * (len(operands) - 1),
        out_specs=(vmem,) * len(outs),
        scratch_shapes=[rows] if call == 2 else [],
        compiler_params=pltpu.CompilerParams(vmem_limit_bytes=32 * 1024 * 1024),
        cost_estimate=pl.CostEstimate(flops=8 * 10**9, bytes_accessed=8 * 1024 * 1024, transcendentals=0),
    )(*operands)


def placed(probe_grad, shape):
    vmem = pl.BlockSpec(memory_space=pltpu.VMEM)
    return pl.pallas_call(
        place,
        out_shape=(jax.ShapeDtypeStruct(shape, jnp.float32),) * 2,
        in_specs=[vmem],
        out_specs=(vmem,) * 2,
        compiler_params=pltpu.CompilerParams(vmem_limit_bytes=4 * 1024 * 1024),
    )(probe_grad)


def flat(block):
    rows, k, parts, columns = block.shape
    split_up = block.reshape(rows, k, parts, columns // 128, 128)
    return split_up.transpose(0, 1, 3, 2, 4).reshape(-1, 128)


def unflat(value, shape):
    rows, k, parts, columns = shape
    return value.reshape(rows, k, columns // 128, parts, 128).transpose(0, 1, 3, 2, 4).reshape(shape)


def partner(value, bits):
    return lax.ppermute(value, "tile", [(i, i ^ bits) for i in range(lax.axis_size("tile"))])


def halved(value):
    return value[:value.shape[0] // 2], value[value.shape[0] // 2:]


def probe_share(probe_grad, shape):
    keep, send = placed(probe_grad, shape)
    total = keep + partner(send, 1)
    for bits in (4, 8):
        keep, send = halved(total)
        total = keep + partner(send, bits)
    keep, send = halved(total)
    return keep + partner(send, 2)


def plan(row_offsets, col_offsets, counts, extent):
    number = jnp.arange(row_offsets.shape[0], dtype=jnp.int32)
    live = number < counts[0]
    key = jnp.where(live, row_offsets, 2 * extent) * row_offsets.shape[0] + number
    rank = jnp.sum((key[None, :] < key[:, None]).astype(jnp.int32), axis=1)
    order = jnp.sum(jnp.where(rank[None, :] == number[:, None], number[None, :], 0), axis=1)
    low = jnp.sum((live & (row_offsets <= extent // 2)).astype(jnp.int32))
    return jnp.concatenate([row_offsets, col_offsets, order, low[None], counts])


def shards(object_slices, probe_field, patterns, row_offsets, col_offsets, counts):
    size = lax.axis_size("tile")
    down = [((i + 1) % size, i) for i in range(size)]
    up = [(i, (i + 1) % size) for i in range(size)]
    own = flat(object_slices)
    low, high = halved(own)
    scalars = plan(row_offsets, col_offsets, counts, patterns.shape[1])

    low = lax.ppermute(low, "tile", down)
    mine = flat(probe_field)
    quarter = jnp.concatenate([mine, partner(mine, 8), partner(mine, 4), partner(mine, 12)], axis=0)
    quarter, patterns, own, scalars = lax.optimization_barrier((quarter, patterns, own, scalars))
    planes, patterns, *mats = prepared(own, patterns)
    near = jnp.concatenate([quarter, partner(quarter, 2)], axis=0)
    high, near, patterns = lax.optimization_barrier((high, near, patterns))
    high = lax.ppermute(high, "tile", down)
    far = partner(near, 1)

    obj, acc, probe, probe_grad = terms(0, scalars, patterns, mats, planes, low, near, far)
    obj, acc, probe_grad, high = terms(1, scalars, patterns, mats, high, obj, acc, probe, probe_grad)
    high = lax.ppermute(high, "tile", up)
    own_grad, low, probe_grad = terms(2, scalars, patterns, mats, obj, acc, probe, probe_grad)

    high, low = lax.optimization_barrier((high, low))
    low = lax.ppermute(low, "tile", up)
    probe_sum = lax.cond(
        counts[0] > 0,
        lambda grad: probe_share(grad, near.shape),
        lambda grad: jnp.zeros((near.shape[0] // 8, near.shape[1]), jnp.float32),
        probe_grad)
    object_grad = own_grad + jnp.concatenate([low, high], axis=0)
    return unflat(object_grad, object_slices.shape), unflat(probe_sum, probe_field.shape)


def solution(mesh):
    in_specs = (
        P(("groups", "tile"), None, None, None),
        P(("groups", "tile"), None, None, None),
        P(("groups", "tile"), None, None),
        P(("groups", "tile")),
        P(("groups", "tile")),
        P(("groups", "tile")),
    )
    out_specs = (P(("groups", "tile"), None, None, None), P(("groups", "tile"), None, None, None))
    return jax.shard_map(shards, mesh=mesh, in_specs=in_specs, out_specs=out_specs, check_vma=False)
```

profile of v0, /device:TPU:6, one launch (start us, length us, event | category | flops | bytes accessed | tf_op | source)
XLA Modules:
  0.0 59.2 jit_solution(12557324529106296652)
XLA Ops:
  0.6 0.0 copy-start.4
  0.6 3.7 %collective-permute-start.6 = (f32[32,128]{1,0:T(8,128)}, f32[32,128]{1,0:T(8,128)S(1)}, u32[]{:S(2)}, u32[]{:S(2)}) collective-permute-start(f32[32,128]{1,0:T(8,128)} %bitcast.24), channel_id=1, source_target_pairs={{0,12},{1,13},{2,14},{3,15},{4,8},{5,9},{6,10},{7,11},{8,4},{9,5},... | collective-permute-start | bytes 49160 | tf_op jit(solution)/shard_map/ppermute | solution.py:352
  4.3 0.0 collective-permute-start.5
  4.3 0.8 %collective-permute-start.4 = (f32[32,128]{1,0:T(8,128)}, f32[32,128]{1,0:T(8,128)S(1)}, u32[]{:S(2)}, u32[]{:S(2)}) collective-permute-start(f32[32,128]{1,0:T(8,128)} %bitcast.26), channel_id=1, source_target_pairs={{0,8},{1,9},{2,10},{3,11},{4,12},{5,13},{6,14},{7,15},{8,0},{9,1},... | collective-permute-start | bytes 49160 | tf_op jit(solution)/shard_map/ppermute | solution.py:352
  5.7 1.3 %fusion.2 = (s32[]{:T(128)}, s32[16]{0:T(128)S(1)}) fusion(s32[16]{0:T(128)} %param.12, s32[]{:T(128)} %bitcast.16), kind=kLoop, calls=%fused_computation.13 | loop fusion | flops 127 | bytes 136 | tf_op jit(solution)/shard_map/reduce_sum | solution.py:375
  7.0 0.2 convert_reduce_fusion
  7.2 0.1 select_reduce_fusion
  7.3 0.0 copy-start.5
  7.3 0.0 copy-start.6
  7.4 0.6 %copy-done.5 = s32[16]{0:T(128)S(1)} copy-done((s32[16]{0:T(128)S(1)}, s32[16]{0:T(128)}, u32[]{:S(2)}) %copy-start.5) | copy-done | bytes 88
  8.0 0.0 copy-done.6
  8.0 0.7 %concatenate.13.scalars_ref = s32[50]{0:T(128)S(1)} concatenate(s32[16]{0:T(128)S(1)} %copy-done.5, s32[16]{0:T(128)S(1)} %copy-done.6, s32[16]{0:T(128)S(1)} %select_reduce_fusion, s32[1]{0:T(128)} %bitcast.6, s32[1]{0:T(128)} %copy.15), dimensions={0} | concatenate | bytes 400 | tf_op jit(solution)/shard_map/concatenate | solution.py:376
  8.7 0.0 collective-permute-done.6
  8.7 0.0 collective-permute-done.5
  8.7 0.4 collective-permute-done.4
  9.2 0.0 copy-done.4
  9.2 0.6 %collective-permute-start.7 = (f32[128,128]{1,0:T(8,128)S(1)}, f32[128,128]{1,0:T(8,128)S(1)}, u32[]{:S(2)}, u32[]{:S(2)}) collective-permute-start(f32[128,128]{1,0:T(8,128)S(1)} %pad_maximum_fusion.1), channel_id=1, source_target_pairs={{0,2},{1,3},{2,0},{3,1},{4,6},{5,7},{6,4},{7,5},{8,10},{9,11},{10,... | collective-permute-start | bytes 196616 | tf_op jit(solution)/shard_map/ppermute | solution.py:352
  9.8 1.2 %fusion.3 = (f32[64,2,2,2,128]{4,3,2,1,0:T(2,128)S(1)}, f32[64,2,2,2,128]{4,3,2,1,0:T(2,128)S(1)}) fusion(f32[128,2,2,2,128]{4,3,2,1,0:T(2,128)} %bitcast.18), kind=kLoop, calls=%fused_computation.14 | loop fusion | bytes 1048576 | tf_op jit(solution)/shard_map/slice | solution.py:356
  11.0 0.1 collective-permute-start.9
  11.1 0.0 copy-done
  11.1 0.0 copy-start.1
  11.1 1.2 %copy-done.1 = f32[16,128,128]{2,1,0:T(8,128)S(1)} copy-done((f32[16,128,128]{2,1,0:T(8,128)S(1)}, f32[16,128,128]{2,1,0:T(8,128)}, u32[]{:S(2)}) %copy-start.1) | copy-done | bytes 1048600
  12.3 1.1 %copy-done.2 = f32[12,128,128]{2,1,0:T(8,128)S(1)} copy-done((f32[12,128,128]{2,1,0:T(8,128)S(1)}, f32[12,128,128]{2,1,0:T(8,128)}, u32[]{:S(2)}) %copy-start.2) | copy-done | bytes 786456
  13.4 0.6 shard_map.86
  14.0 0.0 collective-permute-done.7
  14.0 0.6 collective-permute-start.10
  14.6 2.6 %collective-permute-start.8 = (f32[512,128]{1,0:T(8,128)S(1)}, f32[512,128]{1,0:T(8,128)S(1)}, u32[]{:S(2)}, u32[]{:S(2)}) collective-permute-start(f32[512,128]{1,0:T(8,128)S(1)} %bitcast.21), channel_id=1, source_target_pairs={{1,0},{2,1},{3,2},{4,3},{5,4},{6,5},{7,6},{8,7},{9,8},{10,9},{11,1... | collective-permute-start | bytes 786440 | tf_op jit(solution)/shard_map/ppermute | solution.py:394
  17.2 0.0 collective-permute-done.10.refs_3_
  17.2 0.0 collective-permute-done.9.refs_1_
  17.2 0.7 %shard_map.87 = (f32[8,256,128]{2,1,0:T(8,128)S(1)}, f32[8,256,128]{2,1,0:T(8,128)S(1)}, f32[4,128,128]{2,1,0:T(8,128)S(1)}, f32[4,128,128]{2,1,0:T(8,128)S(1)}) custom-call(s32[50]{0:T(128)S(1)} %concatenate.13.scalars_ref, f32[16,128,128]{2,1,0:T(8,128)S(1)} %get-tuple-element.38.patterns_ref, bf16[8,256,256]{2,1,0:T(8,128)(2,1)S(1)} %get-tuple-element.39.mats_ref, ...), custom_call_target="tpu_custom_call" | custom-call | flops 8000000000 | bytes 8388608 | tf_op jit(solution)/shard_map/pallas_call | solution.py:318
  17.9 3.1 %collective-permute-done.8.refs_0_ = f32[512,128]{1,0:T(8,128)S(1)} collective-permute-done((f32[512,128]{1,0:T(8,128)S(1)}, f32[512,128]{1,0:T(8,128)S(1)}, u32[]{:S(2)}, u32[]{:S(2)}) %collective-permute-start.8) | collective-permute-done | bytes 262176 | tf_op jit(solution)/shard_map/ppermute | solution.py:394
  21.1 3.6 %shard_map.88 = (f32[8,256,128]{2,1,0:T(8,128)S(1)}, f32[8,256,128]{2,1,0:T(8,128)S(1)}, f32[4,128,128]{2,1,0:T(8,128)S(1)}, f32[512,128]{1,0:T(8,128)S(1)}) custom-call(s32[50]{0:T(128)S(1)} %concatenate.13.scalars_ref, f32[16,128,128]{2,1,0:T(8,128)S(1)} %get-tuple-element.38.patterns_ref, bf16[8,256,256]{2,1,0:T(8,128)(2,1)S(1)} %get-tuple-element.39.mats_ref, ...), custom_call_target="tpu_custom_call" | custom-call | flops 8000000000 | bytes 8388608 | tf_op jit(solution)/shard_map/pallas_call | solution.py:318
  24.7 12.1 %collective-permute-start.11 = (f32[512,128]{1,0:T(8,128)S(1)}, f32[512,128]{1,0:T(8,128)S(1)}, u32[]{:S(2)}, u32[]{:S(2)}) collective-permute-start(f32[512,128]{1,0:T(8,128)S(1)} %get-tuple-element.52), channel_id=1, source_target_pairs={{0,1},{1,2},{2,3},{3,4},{4,5},{5,6},{6,7},{7,8},{8,9},{9,10},{10,1... | collective-permute-start | bytes 786440 | tf_op jit(solution)/shard_map/ppermute | solution.py:399
  36.8 0.8 %shard_map.89 = (f32[1024,128]{1,0:T(8,128)S(1)}, f32[512,128]{1,0:T(8,128)S(1)}, f32[4,128,128]{2,1,0:T(8,128)S(1)}) custom-call(s32[50]{0:T(128)S(1)} %concatenate.13.scalars_ref, f32[16,128,128]{2,1,0:T(8,128)S(1)} %get-tuple-element.38.patterns_ref, bf16[8,256,256]{2,1,0:T(8,128)(2,1)S(1)} %get-tuple-element.39.mats_ref, ...), custom_call_target="tpu_custom_call" | custom-call | flops 8000000000 | bytes 8388608 | tf_op jit(solution)/shard_map/pallas_call | solution.py:318
  37.6 0.3 collective-permute-done.11
  38.0 2.2 %collective-permute-start.12 = (f32[512,128]{1,0:T(8,128)S(1)}, f32[512,128]{1,0:T(8,128)S(1)}, u32[]{:S(2)}, u32[]{:S(2)}) collective-permute-start(f32[512,128]{1,0:T(8,128)S(1)} %get-tuple-element.54), channel_id=1, source_target_pairs={{0,1},{1,2},{2,3},{3,4},{4,5},{5,6},{6,7},{7,8},{8,9},{9,10},{10,1... | collective-permute-start | bytes 786440 | tf_op jit(solution)/shard_map/ppermute | solution.py:403
  40.1 18.2 %conditional.1 = (f32[8,2,2,128]{3,2,1,0:T(2,128)S(1)}) conditional(s32[]{:T(128)} %convert_element_type.11, () %tuple.22, f32[4,128,128]{2,1,0:T(8,128)S(1)} %get-tuple-element.56), branch_computations={%region_3.4_spmd, %region_4.5_spmd} | conditional | flops 61440 | bytes 1949864 | solution.py:404
  40.2 3.4 %collective-permute-start = (f32[256,128]{1,0:T(8,128)S(1)}, f32[256,128]{1,0:T(8,128)S(1)}, u32[]{:S(2)}, u32[]{:S(2)}) collective-permute-start(f32[256,128]{1,0:T(8,128)S(1)} %get-tuple-element.6), channel_id=1, source_target_pairs={{0,1},{1,0},{2,3},{3,2},{4,5},{5,4},{6,7},{7,6},{8,9},{9,8},{10,11... | collective-permute-start | bytes 393224 | tf_op jit(solution)/shard_map/cond/branch_1_fun/ppermute | solution.py:352
  43.6 1.0 %collective-permute-done = f32[256,128]{1,0:T(8,128)S(1)} collective-permute-done((f32[256,128]{1,0:T(8,128)S(1)}, f32[256,128]{1,0:T(8,128)S(1)}, u32[]{:S(2)}, u32[]{:S(2)}) %collective-permute-start) | collective-permute-done | bytes 131104 | tf_op jit(solution)/shard_map/cond/branch_1_fun/ppermute | solution.py:352
  44.6 0.1 collective-permute-start.1
  44.7 4.3 %collective-permute-done.1 = f32[128,128]{1,0:T(8,128)S(1)} collective-permute-done((f32[128,128]{1,0:T(8,128)S(1)}, f32[128,128]{1,0:T(8,128)S(1)}, u32[]{:S(2)}, u32[]{:S(2)}) %collective-permute-start.1) | collective-permute-done | bytes 65568 | tf_op jit(solution)/shard_map/cond/branch_1_fun/ppermute | solution.py:352
  49.1 0.1 collective-permute-start.2
  49.2 5.3 %collective-permute-done.2 = f32[64,128]{1,0:T(8,128)S(1)} collective-permute-done((f32[64,128]{1,0:T(8,128)S(1)}, f32[64,128]{1,0:T(8,128)S(1)}, u32[]{:S(2)}, u32[]{:S(2)}) %collective-permute-start.2) | collective-permute-done | bytes 32800 | tf_op jit(solution)/shard_map/cond/branch_1_fun/ppermute | solution.py:352
  54.5 0.1 collective-permute-start.3
  54.6 3.7 %collective-permute-done.3 = f32[32,128]{1,0:T(8,128)S(1)} collective-permute-done((f32[32,128]{1,0:T(8,128)S(1)}, f32[32,128]{1,0:T(8,128)S(1)}, u32[]{:S(2)}, u32[]{:S(2)}) %collective-permute-start.3) | collective-permute-done | bytes 16416 | tf_op jit(solution)/shard_map/cond/branch_1_fun/ppermute | solution.py:352
  58.3 0.0 collective-permute-done.12
  58.3 0.8 %maximum_add_fusion = f32[1024,128]{1,0:T(8,128)} fusion(f32[1024,128]{1,0:T(8,128)S(1)} %get-tuple-element.51, f32[512,128]{1,0:T(8,128)S(1)} %collective-permute-done.11, f32[512,128]{1,0:T(8,128)S(1)} %collective-permute-done.12), kind=kLoop, calls=%fused_computation.3 | loop fusion | flops 262144 | bytes 1572864 | tf_op jit(solution)/shard_map/add | solution.py:409
  59.2 0.0 copy-done.3
  (13 shorter events, 0.1 us)
Async XLA Ops:
  0.6 8.5 %copy-start.4 = (f32[8,2,2,128]{3,2,1,0:T(2,128)S(1)}, f32[8,2,2,128]{3,2,1,0:T(2,128)}, u32[]{:S(2)}) copy-start(f32[8,2,2,128]{3,2,1,0:T(2,128)} %param.10) | copy-start | bytes 49156
  0.6 8.1 %collective-permute-start.6 = (f32[32,128]{1,0:T(8,128)}, f32[32,128]{1,0:T(8,128)S(1)}, u32[]{:S(2)}, u32[]{:S(2)}) collective-permute-start(f32[32,128]{1,0:T(8,128)} %bitcast.24), channel_id=1, source_target_pairs={{0,12},{1,13},{2,14},{3,15},{4,8},{5,9},{6,10},{7,11},{8,4},{9,5},... | collective-permute-start | bytes 49160 | tf_op jit(solution)/shard_map/ppermute | solution.py:352
  4.3 4.4 %collective-permute-start.5 = (f32[32,128]{1,0:T(8,128)}, f32[32,128]{1,0:T(8,128)S(1)}, u32[]{:S(2)}, u32[]{:S(2)}) collective-permute-start(f32[32,128]{1,0:T(8,128)} %bitcast.25), channel_id=1, source_target_pairs={{0,4},{1,5},{2,6},{3,7},{4,0},{5,1},{6,2},{7,3},{8,12},{9,13},{10,... | collective-permute-start | bytes 49160 | tf_op jit(solution)/shard_map/ppermute | solution.py:352
  4.3 4.8 %collective-permute-start.4 = (f32[32,128]{1,0:T(8,128)}, f32[32,128]{1,0:T(8,128)S(1)}, u32[]{:S(2)}, u32[]{:S(2)}) collective-permute-start(f32[32,128]{1,0:T(8,128)} %bitcast.26), channel_id=1, source_target_pairs={{0,8},{1,9},{2,10},{3,11},{4,12},{5,13},{6,14},{7,15},{8,0},{9,1},... | collective-permute-start | bytes 49160 | tf_op jit(solution)/shard_map/ppermute | solution.py:352
  7.3 0.7 %copy-start.5 = (s32[16]{0:T(128)S(1)}, s32[16]{0:T(128)}, u32[]{:S(2)}) copy-start(s32[16]{0:T(128)} %param.12) | copy-start | bytes 196
  7.3 0.7 %copy-start.6 = (s32[16]{0:T(128)S(1)}, s32[16]{0:T(128)}, u32[]{:S(2)}) copy-start(s32[16]{0:T(128)} %param.13) | copy-start | bytes 196
  9.2 4.8 %collective-permute-start.7 = (f32[128,128]{1,0:T(8,128)S(1)}, f32[128,128]{1,0:T(8,128)S(1)}, u32[]{:S(2)}, u32[]{:S(2)}) collective-permute-start(f32[128,128]{1,0:T(8,128)S(1)} %pad_maximum_fusion.1), channel_id=1, source_target_pairs={{0,2},{1,3},{2,0},{3,1},{4,6},{5,7},{6,4},{7,5},{8,10},{9,11},{10,... | collective-permute-start | bytes 196616 | tf_op jit(solution)/shard_map/ppermute | solution.py:352
  9.8 1.3 %copy-start = (f32[128,2,2,256]{3,2,1,0:T(2,128)S(1)}, f32[128,2,2,256]{3,2,1,0:T(2,128)}, u32[]{:S(2)}) copy-start(f32[128,2,2,256]{3,2,1,0:T(2,128)} %param.9) | copy-start | bytes 1572868
  11.0 6.2 %collective-permute-start.9 = (f32[512,128]{1,0:T(8,128)S(1)}, f32[512,128]{1,0:T(8,128)S(1)}, u32[]{:S(2)}, u32[]{:S(2)}) collective-permute-start(f32[512,128]{1,0:T(8,128)S(1)} %bitcast.22), channel_id=1, source_target_pairs={{1,0},{2,1},{3,2},{4,3},{5,4},{6,5},{7,6},{8,7},{9,8},{10,9},{11,1... | collective-permute-start | bytes 786440 | tf_op jit(solution)/shard_map/ppermute | solution.py:387
  11.1 1.2 %copy-start.1 = (f32[16,128,128]{2,1,0:T(8,128)S(1)}, f32[16,128,128]{2,1,0:T(8,128)}, u32[]{:S(2)}) copy-start(f32[16,128,128]{2,1,0:T(8,128)} %patterns_ref) | copy-start | bytes 3145732
  12.3 1.1 %copy-start.2 = (f32[12,128,128]{2,1,0:T(8,128)S(1)}, f32[12,128,128]{2,1,0:T(8,128)}, u32[]{:S(2)}) copy-start(f32[12,128,128]{2,1,0:T(8,128)} %constant.12.clone.factors_ref) | copy-start | bytes 2359300
  14.0 3.2 %collective-permute-start.10 = (f32[256,128]{1,0:T(8,128)S(1)}, f32[256,128]{1,0:T(8,128)S(1)}, u32[]{:S(2)}, u32[]{:S(2)}) collective-permute-start(f32[256,128]{1,0:T(8,128)S(1)} %pad_maximum_fusion.refs_2_), channel_id=1, source_target_pairs={{0,1},{1,0},{2,3},{3,2},{4,5},{5,4},{6,7},{7,6},{8,9},{9,8},{10,11... | collective-permute-start | bytes 393224 | tf_op jit(solution)/shard_map/ppermute | solution.py:352
  14.6 6.5 %collective-permute-start.8 = (f32[512,128]{1,0:T(8,128)S(1)}, f32[512,128]{1,0:T(8,128)S(1)}, u32[]{:S(2)}, u32[]{:S(2)}) collective-permute-start(f32[512,128]{1,0:T(8,128)S(1)} %bitcast.21), channel_id=1, source_target_pairs={{1,0},{2,1},{3,2},{4,3},{5,4},{6,5},{7,6},{8,7},{9,8},{10,9},{11,1... | collective-permute-start | bytes 786440 | tf_op jit(solution)/shard_map/ppermute | solution.py:394
  24.7 13.3 %collective-permute-start.11 = (f32[512,128]{1,0:T(8,128)S(1)}, f32[512,128]{1,0:T(8,128)S(1)}, u32[]{:S(2)}, u32[]{:S(2)}) collective-permute-start(f32[512,128]{1,0:T(8,128)S(1)} %get-tuple-element.52), channel_id=1, source_target_pairs={{0,1},{1,2},{2,3},{3,4},{4,5},{5,6},{6,7},{7,8},{8,9},{9,10},{10,1... | collective-permute-start | bytes 786440 | tf_op jit(solution)/shard_map/ppermute | solution.py:399
  38.0 20.3 %collective-permute-start.12 = (f32[512,128]{1,0:T(8,128)S(1)}, f32[512,128]{1,0:T(8,128)S(1)}, u32[]{:S(2)}, u32[]{:S(2)}) collective-permute-start(f32[512,128]{1,0:T(8,128)S(1)} %get-tuple-element.54), channel_id=1, source_target_pairs={{0,1},{1,2},{2,3},{3,4},{4,5},{5,6},{6,7},{7,8},{8,9},{9,10},{10,1... | collective-permute-start | bytes 786440 | tf_op jit(solution)/shard_map/ppermute | solution.py:403
  40.2 4.4 %collective-permute-start = (f32[256,128]{1,0:T(8,128)S(1)}, f32[256,128]{1,0:T(8,128)S(1)}, u32[]{:S(2)}, u32[]{:S(2)}) collective-permute-start(f32[256,128]{1,0:T(8,128)S(1)} %get-tuple-element.6), channel_id=1, source_target_pairs={{0,1},{1,0},{2,3},{3,2},{4,5},{5,4},{6,7},{7,6},{8,9},{9,8},{10,11... | collective-permute-start | bytes 393224 | tf_op jit(solution)/shard_map/cond/branch_1_fun/ppermute | solution.py:352
  44.6 4.4 %collective-permute-start.1 = (f32[128,128]{1,0:T(8,128)S(1)}, f32[128,128]{1,0:T(8,128)S(1)}, u32[]{:S(2)}, u32[]{:S(2)}) collective-permute-start(f32[128,128]{1,0:T(8,128)S(1)} %slice.35), channel_id=1, source_target_pairs={{0,4},{1,5},{2,6},{3,7},{4,0},{5,1},{6,2},{7,3},{8,12},{9,13},{10,... | collective-permute-start | bytes 196616 | tf_op jit(solution)/shard_map/cond/branch_1_fun/ppermute | solution.py:352
  49.1 5.4 %collective-permute-start.2 = (f32[64,128]{1,0:T(8,128)S(1)}, f32[64,128]{1,0:T(8,128)S(1)}, u32[]{:S(2)}, u32[]{:S(2)}) collective-permute-start(f32[64,128]{1,0:T(8,128)S(1)} %slice.37), channel_id=1, source_target_pairs={{0,8},{1,9},{2,10},{3,11},{4,12},{5,13},{6,14},{7,15},{8,0},{9,1},... | collective-permute-start | bytes 98312 | tf_op jit(solution)/shard_map/cond/branch_1_fun/ppermute | solution.py:352
  54.5 3.8 %collective-permute-start.3 = (f32[32,128]{1,0:T(8,128)S(1)}, f32[32,128]{1,0:T(8,128)S(1)}, u32[]{:S(2)}, u32[]{:S(2)}) collective-permute-start(f32[32,128]{1,0:T(8,128)S(1)} %slice.39), channel_id=1, source_target_pairs={{0,2},{1,3},{2,0},{3,1},{4,6},{5,7},{6,4},{7,5},{8,10},{9,11},{10,... | collective-permute-start | bytes 49160 | tf_op jit(solution)/shard_map/cond/branch_1_fun/ppermute | solution.py:352
  58.3 0.9 %copy-start.3 = (f32[8,2,2,128]{3,2,1,0:T(2,128)}, f32[8,2,2,128]{3,2,1,0:T(2,128)S(1)}, u32[]{:S(2)}) copy-start(f32[8,2,2,128]{3,2,1,0:T(2,128)S(1)} %get-tuple-element.61) | copy-start | bytes 49156
where the time goes:
time: 58.5 us; the launch traced here: 59.2 us
  starting transfers between devices  26.2 us (45%)
  waiting for transfers between devices  18.3 us (31%)
  Pallas kernels  5.77 us (10%)
  local copies, waits for them, and re-layouts  4.99 us (9%)
  other arithmetic  2.49 us (4%)
  between operations  1.4 us (2%)
    ppermute x9, waiting for transfers between devices, partner(): lax.ppermute(value, 'tile', [(i, i ^ bits) for i in range(lax.axis_size('...  14.8 us
    ppermute x1, starting transfers between devices, shards(): high = lax.ppermute(high, 'tile', up)  12.1 us
    ppermute x9, starting transfers between devices, partner(): lax.ppermute(value, 'tile', [(i, i ^ bits) for i in range(lax.axis_size('...  9.26 us
    pallas_call x3, Pallas kernels, terms(): pl.pallas_call(functools.partial(kernel, call), out_shape=outs, in_specs=...  5.18 us
    ppermute x1, waiting for transfers between devices, shards(): high = lax.ppermute(high, 'tile', down)  3.14 us
    unnamed x14, local copies, waits for them, and re-layouts  3.03 us
    ppermute x1, starting transfers between devices, shards(): high = lax.ppermute(high, 'tile', down)  2.6 us
    ppermute x1, starting transfers between devices, shards(): low = lax.ppermute(low, 'tile', up)  2.16 us
  transfers between devices with their start and end apart: 13, of which 7 were waited for; matrix products, arithmetic and copies ran while one was open for 6% of the time, Pallas kernels for 4%

commit v1 on v0

--- a/solution.py
+++ b/solution.py
@@ -94,10 +94,11 @@
     share = extent // GROUP_DEV
     member = lax.rem(lax.axis_index("tile"), GROUP_DEV)
     for odd, ref in enumerate((keep_out, send_out)):
-        for block, order in enumerate(BACK):
+        for block in range(GROUP_DEV // 2):
+            there = lax.bitwise_xor(lax.rem(member + block // 2 * 4, GROUP_DEV), 2 * (block % 2) + odd)
             for k in range(lanes):
                 rows = pl.ds(block * share * lanes + k, share, stride=lanes)
-                ref[rows, :] = probe_ref[k, member_rows(member, order + odd, share), :]
+                ref[rows, :] = probe_ref[k, pl.ds(pl.multiple_of(there * share, share), share), :]
 
 
 def kernel(call, scalars_ref, patterns_ref, mats_ref, half_ref, *refs):
@@ -356,14 +357,10 @@
     return value[:value.shape[0] // 2], value[value.shape[0] // 2:]
 
 
-def probe_share(probe_grad, shape):
-    keep, send = placed(probe_grad, shape)
-    total = keep + partner(send, 1)
-    for bits in (4, 8):
-        keep, send = halved(total)
-        total = keep + partner(send, bits)
-    keep, send = halved(total)
-    return keep + partner(send, 2)
+def places_on(value, distance):
+    members = range(lax.axis_size("tile"))
+    return lax.ppermute(value, "tile", [
+        (i, i // GROUP_DEV * GROUP_DEV + (i + distance) % GROUP_DEV) for i in members])
 
 
 def plan(row_offsets, col_offsets, counts, extent):
@@ -382,15 +379,16 @@
     up = [(i, (i + 1) % size) for i in range(size)]
     own = flat(object_slices)
     low, high = halved(own)
-    scalars = plan(row_offsets, col_offsets, counts, patterns.shape[1])
 
     low = lax.ppermute(low, "tile", down)
     mine = flat(probe_field)
     quarter = jnp.concatenate([mine, partner(mine, 8), partner(mine, 4), partner(mine, 12)], axis=0)
-    quarter, patterns, own, scalars = lax.optimization_barrier((quarter, patterns, own, scalars))
+    quarter, patterns, own, offsets = lax.optimization_barrier(
+        (quarter, patterns, own, (row_offsets, col_offsets, counts)))
+    scalars = plan(*offsets, patterns.shape[1])
     planes, patterns, *mats = prepared(own, patterns)
     near = jnp.concatenate([quarter, partner(quarter, 2)], axis=0)
-    high, near, patterns = lax.optimization_barrier((high, near, patterns))
+    high, near, patterns, scalars = lax.optimization_barrier((high, near, patterns, scalars))
     high = lax.ppermute(high, "tile", down)
     far = partner(near, 1)
 
@@ -399,15 +397,17 @@
     high = lax.ppermute(high, "tile", up)
     own_grad, low, probe_grad = terms(2, scalars, patterns, mats, obj, acc, probe, probe_grad)
 
-    high, low = lax.optimization_barrier((high, low))
     low = lax.ppermute(low, "tile", up)
-    probe_sum = lax.cond(
-        counts[0] > 0,
-        lambda grad: probe_share(grad, near.shape),
-        lambda grad: jnp.zeros((near.shape[0] // 8, near.shape[1]), jnp.float32),
-        probe_grad)
+    keep, send = placed(probe_grad, near.shape)
+    total = keep + partner(send, 1)
+    high, total = lax.optimization_barrier((high, total))
+    blocks = jnp.split(total, 4, axis=0)
+    total = blocks[0] + sum(places_on(block, 4 * k) for k, block in enumerate(blocks) if k > 0)
+    keep, send = halved(total)
+    send = partner(send, 2)
+    low, send = lax.optimization_barrier((low, send))
     object_grad = own_grad + jnp.concatenate([low, high], axis=0)
-    return unflat(object_grad, object_slices.shape), unflat(probe_sum, probe_field.shape)
+    return unflat(object_grad, object_slices.shape), unflat(keep + send, probe_field.shape)
 
 
 def solution(mesh):

time: 58.5 us -> 55.3 us (0.945)
  the two profiles are of different devices: /device:TPU:6 before, /device:TPU:0 now
where the time goes in v1:
time: 55.3 us; the launch traced here: 55 us
  starting transfers between devices  19.5 us (35%)
  waiting for transfers between devices  18.6 us (34%)
  Pallas kernels  7.38 us (13%)
  local copies, waits for them, and re-layouts  5.63 us (10%)
  other arithmetic  2.44 us (4%)
  between operations  1.44 us (3%)
    pallas_call x3, Pallas kernels, terms(): pl.pallas_call(functools.partial(kernel, call), out_shape=outs, in_specs=...  6.77 us
    ppermute x7, starting transfers between devices, partner(): lax.ppermute(value, 'tile', [(i, i ^ bits) for i in range(lax.axis_size('...  6.49 us
    ppermute x3, waiting for transfers between devices, places_on(): lax.ppermute(value, 'tile', [(i, i // GROUP_DEV * GROUP_DEV + (i + distan...  5.71 us
    ppermute x1, waiting for transfers between devices, shards(): high = lax.ppermute(high, 'tile', up)  4.68 us
    ppermute x3, starting transfers between devices, places_on(): lax.ppermute(value, 'tile', [(i, i // GROUP_DEV * GROUP_DEV + (i + distan...  4.59 us
    unnamed x12, local copies, waits for them, and re-layouts  3.67 us
    ppermute x1, starting transfers between devices, shards(): high = lax.ppermute(high, 'tile', down)  3.45 us
    ppermute x1, starting transfers between devices, shards(): low = lax.ppermute(low, 'tile', down)  3.32 us
  transfers between devices with their start and end apart: 14, of which 8 were waited for; matrix products, arithmetic and copies ran while one was open for 5% of the time, Pallas kernels for 4%

profile of v1, /device:TPU:0, one launch (start us, length us, event | category | flops | bytes accessed | tf_op | source)
XLA Modules:
  0.0 55.0 jit_solution(1064252762717571971)
XLA Ops:
  0.6 5.1 %collective-permute-start.2 = (f32[32,128]{1,0:T(8,128)}, f32[32,128]{1,0:T(8,128)S(1)}, u32[]{:S(2)}, u32[]{:S(2)}) collective-permute-start(f32[32,128]{1,0:T(8,128)} %bitcast.23), channel_id=1, source_target_pairs={{0,12},{1,13},{2,14},{3,15},{4,8},{5,9},{6,10},{7,11},{8,4},{9,5},... | collective-permute-start | bytes 49160 | tf_op jit(solution)/shard_map/ppermute | solution.py:353
  5.7 0.0 collective-permute-start.1
  5.7 0.6 %collective-permute-start = (f32[32,128]{1,0:T(8,128)}, f32[32,128]{1,0:T(8,128)S(1)}, u32[]{:S(2)}, u32[]{:S(2)}) collective-permute-start(f32[32,128]{1,0:T(8,128)} %bitcast.25), channel_id=1, source_target_pairs={{0,8},{1,9},{2,10},{3,11},{4,12},{5,13},{6,14},{7,15},{8,0},{9,1},... | collective-permute-start | bytes 49160 | tf_op jit(solution)/shard_map/ppermute | solution.py:353
  6.4 0.0 copy-start.3
  6.4 0.0 copy-start
  6.4 1.2 %fusion.3 = (f32[64,2,2,2,128]{4,3,2,1,0:T(2,128)S(1)}, f32[64,2,2,2,128]{4,3,2,1,0:T(2,128)S(1)}) fusion(f32[128,2,2,2,128]{4,3,2,1,0:T(2,128)} %bitcast.17), kind=kLoop, calls=%fused_computation.13 | loop fusion | bytes 1048576 | tf_op jit(solution)/shard_map/slice | solution.py:357
  7.6 3.3 %collective-permute-start.5 = (f32[512,128]{1,0:T(8,128)S(1)}, f32[512,128]{1,0:T(8,128)S(1)}, u32[]{:S(2)}, u32[]{:S(2)}) collective-permute-start(f32[512,128]{1,0:T(8,128)S(1)} %bitcast.21), channel_id=1, source_target_pairs={{1,0},{2,1},{3,2},{4,3},{5,4},{6,5},{7,6},{8,7},{9,8},{10,9},{11,1... | collective-permute-start | bytes 786440 | tf_op jit(solution)/shard_map/ppermute | solution.py:383
  11.6 0.0 collective-permute-done.2
  11.6 0.0 collective-permute-done.1
  11.6 0.0 collective-permute-done
  11.6 0.0 copy-done.3
  11.7 0.0 copy-start.4
  11.7 0.6 %copy-done.4 = s32[16]{0:T(128)S(1)} copy-done((s32[16]{0:T(128)S(1)}, s32[16]{0:T(128)}, u32[]{:S(2)}) %copy-start.4) | copy-done | bytes 88
  12.3 0.6 %fusion.2 = (s32[]{:T(128)}, s32[16]{0:T(128)S(1)}) fusion(s32[16]{0:T(128)S(1)} %copy-done.4, s32[]{:T(128)} %bitcast.16), kind=kLoop, calls=%fused_computation.12 | loop fusion | flops 127 | bytes 136 | tf_op jit(solution)/shard_map/reduce_sum | solution.py:372
  12.9 0.2 convert_reduce_fusion
  13.1 0.5 collective-permute-start.3
  13.6 0.1 select_reduce_fusion
  13.7 0.7 %copy-done.5 = s32[16]{0:T(128)S(1)} copy-done((s32[16]{0:T(128)S(1)}, s32[16]{0:T(128)}, u32[]{:S(2)}) %copy-start.5) | copy-done | bytes 88
  14.4 0.7 %concatenate.14.scalars_ref = s32[50]{0:T(128)S(1)} concatenate(s32[16]{0:T(128)S(1)} %copy-done.4, s32[16]{0:T(128)S(1)} %copy-done.5, s32[16]{0:T(128)S(1)} %select_reduce_fusion, s32[1]{0:T(128)} %bitcast.7, s32[1]{0:T(128)} %copy.13), dimensions={0} | concatenate | bytes 400 | tf_op jit(solution)/shard_map/concatenate | solution.py:373
  15.1 0.0 copy-done
  15.1 1.2 %copy-done.1 = f32[16,128,128]{2,1,0:T(8,128)S(1)} copy-done((f32[16,128,128]{2,1,0:T(8,128)S(1)}, f32[16,128,128]{2,1,0:T(8,128)}, u32[]{:S(2)}) %copy-start.1) | copy-done | bytes 1048600
  16.4 1.1 %copy-done.2 = f32[12,128,128]{2,1,0:T(8,128)S(1)} copy-done((f32[12,128,128]{2,1,0:T(8,128)S(1)}, f32[12,128,128]{2,1,0:T(8,128)}, u32[]{:S(2)}) %copy-start.2) | copy-done | bytes 786456
  17.5 0.6 %shard_map.86 = (f32[8,128,128]{2,1,0:T(8,128)S(1)}, f32[16,128,128]{2,1,0:T(8,128)S(1)}, bf16[8,256,256]{2,1,0:T(8,128)(2,1)S(1)}, bf16[8,256,256]{2,1,0:T(8,128)(2,1)S(1)}) custom-call(f32[1024,128]{1,0:T(8,128)S(1)} %bitcast.18, f32[16,128,128]{2,1,0:T(8,128)S(1)} %copy-done.1, f32[12,128,128]{2,1,0:T(8,128)S(1)} %copy-done.2), custom_call_target="tpu_custom_call" | custom-call | bytes 6291456 | tf_op jit(solution)/shard_map/pallas_call | solution.py:288
  18.1 0.0 collective-permute-done.3
  18.1 0.1 collective-permute-start.6
  18.2 3.4 %collective-permute-start.4 = (f32[512,128]{1,0:T(8,128)S(1)}, f32[512,128]{1,0:T(8,128)S(1)}, u32[]{:S(2)}, u32[]{:S(2)}) collective-permute-start(f32[512,128]{1,0:T(8,128)S(1)} %bitcast.20), channel_id=1, source_target_pairs={{1,0},{2,1},{3,2},{4,3},{5,4},{6,5},{7,6},{8,7},{9,8},{10,9},{11,1... | collective-permute-start | bytes 786440 | tf_op jit(solution)/shard_map/ppermute | solution.py:392
  21.6 0.0 collective-permute-done.6.refs_3_
  21.6 0.0 collective-permute-done.5.refs_1_
  21.6 0.7 %shard_map.87 = (f32[8,256,128]{2,1,0:T(8,128)S(1)}, f32[8,256,128]{2,1,0:T(8,128)S(1)}, f32[4,128,128]{2,1,0:T(8,128)S(1)}, f32[4,128,128]{2,1,0:T(8,128)S(1)}) custom-call(s32[50]{0:T(128)S(1)} %concatenate.14.scalars_ref, f32[16,128,128]{2,1,0:T(8,128)S(1)} %get-tuple-element.41.patterns_ref, bf16[8,256,256]{2,1,0:T(8,128)(2,1)S(1)} %get-tuple-element.42.mats_ref, ...), custom_call_target="tpu_custom_call" | custom-call | flops 8000000000 | bytes 8388608 | tf_op jit(solution)/shard_map/pallas_call | solution.py:319
  22.4 3.1 %collective-permute-done.4.refs_0_ = f32[512,128]{1,0:T(8,128)S(1)} collective-permute-done((f32[512,128]{1,0:T(8,128)S(1)}, f32[512,128]{1,0:T(8,128)S(1)}, u32[]{:S(2)}, u32[]{:S(2)}) %collective-permute-start.4) | collective-permute-done | bytes 262176 | tf_op jit(solution)/shard_map/ppermute | solution.py:392
  25.5 5.2 %shard_map.88 = (f32[8,256,128]{2,1,0:T(8,128)S(1)}, f32[8,256,128]{2,1,0:T(8,128)S(1)}, f32[4,128,128]{2,1,0:T(8,128)S(1)}, f32[512,128]{1,0:T(8,128)S(1)}) custom-call(s32[50]{0:T(128)S(1)} %concatenate.14.scalars_ref, f32[16,128,128]{2,1,0:T(8,128)S(1)} %get-tuple-element.41.patterns_ref, bf16[8,256,256]{2,1,0:T(8,128)(2,1)S(1)} %get-tuple-element.42.mats_ref, ...), custom_call_target="tpu_custom_call" | custom-call | flops 8000000000 | bytes 8388608 | tf_op jit(solution)/shard_map/pallas_call | solution.py:319
  30.7 1.7 %collective-permute-start.8 = (f32[512,128]{1,0:T(8,128)S(1)}, f32[512,128]{1,0:T(8,128)S(1)}, u32[]{:S(2)}, u32[]{:S(2)}) collective-permute-start(f32[512,128]{1,0:T(8,128)S(1)} %get-tuple-element.56), channel_id=1, source_target_pairs={{0,1},{1,2},{2,3},{3,4},{4,5},{5,6},{6,7},{7,8},{8,9},{9,10},{10,1... | collective-permute-start | bytes 786440 | tf_op jit(solution)/shard_map/ppermute | solution.py:397
  32.4 0.8 %shard_map.89 = (f32[1024,128]{1,0:T(8,128)S(1)}, f32[512,128]{1,0:T(8,128)S(1)}, f32[4,128,128]{2,1,0:T(8,128)S(1)}) custom-call(s32[50]{0:T(128)S(1)} %concatenate.14.scalars_ref, f32[16,128,128]{2,1,0:T(8,128)S(1)} %get-tuple-element.41.patterns_ref, bf16[8,256,256]{2,1,0:T(8,128)(2,1)S(1)} %get-tuple-element.42.mats_ref, ...), custom_call_target="tpu_custom_call" | custom-call | flops 8000000000 | bytes 8388608 | tf_op jit(solution)/shard_map/pallas_call | solution.py:319
  33.3 0.1 collective-permute-start.9
  33.4 1.3 %collective-permute-done.9 = f32[256,128]{1,0:T(8,128)S(1)} collective-permute-done((f32[256,128]{1,0:T(8,128)S(1)}, f32[256,128]{1,0:T(8,128)S(1)}, u32[]{:S(2)}, u32[]{:S(2)}) %collective-permute-start.9) | collective-permute-done | bytes 131104 | tf_op jit(solution)/shard_map/ppermute | solution.py:353
  34.7 4.7 %collective-permute-done.8 = f32[512,128]{1,0:T(8,128)S(1)} collective-permute-done((f32[512,128]{1,0:T(8,128)S(1)}, f32[512,128]{1,0:T(8,128)S(1)}, u32[]{:S(2)}, u32[]{:S(2)}) %collective-permute-start.8) | collective-permute-done | bytes 262176 | tf_op jit(solution)/shard_map/ppermute | solution.py:397
  39.4 1.9 %collective-permute-start.11 = (f32[64,128]{1,0:T(8,128)S(1)}, f32[64,128]{1,0:T(8,128)S(1)}, u32[]{:S(2)}, u32[]{:S(2)}) collective-permute-start(f32[64,128]{1,0:T(8,128)S(1)} %get-tuple-element.66), channel_id=1, source_target_pairs={{0,8},{1,9},{2,10},{3,11},{4,12},{5,13},{6,14},{7,15},{8,0},{9,1},... | collective-permute-start | bytes 98312 | tf_op jit(solution)/shard_map/ppermute | solution.py:362
  41.3 2.7 %collective-permute-start.12 = (f32[64,128]{1,0:T(8,128)S(1)}, f32[64,128]{1,0:T(8,128)S(1)}, u32[]{:S(2)}, u32[]{:S(2)}) collective-permute-start(f32[64,128]{1,0:T(8,128)S(1)} %get-tuple-element.67), channel_id=1, source_target_pairs={{0,12},{1,13},{2,14},{3,15},{4,0},{5,1},{6,2},{7,3},{8,4},{9,5},{1... | collective-permute-start | bytes 98312 | tf_op jit(solution)/shard_map/ppermute | solution.py:362
  44.0 0.0 collective-permute-start.10
  44.0 0.0 collective-permute-start.7
  44.0 0.3 collective-permute-done.11
  44.3 1.3 %collective-permute-done.12 = f32[64,128]{1,0:T(8,128)S(1)} collective-permute-done((f32[64,128]{1,0:T(8,128)S(1)}, f32[64,128]{1,0:T(8,128)S(1)}, u32[]{:S(2)}, u32[]{:S(2)}) %collective-permute-start.12) | collective-permute-done | bytes 32800 | tf_op jit(solution)/shard_map/ppermute | solution.py:362
  45.6 4.1 %collective-permute-done.10 = f32[64,128]{1,0:T(8,128)S(1)} collective-permute-done((f32[64,128]{1,0:T(8,128)S(1)}, f32[64,128]{1,0:T(8,128)S(1)}, u32[]{:S(2)}, u32[]{:S(2)}) %collective-permute-start.10) | collective-permute-done | bytes 32800 | tf_op jit(solution)/shard_map/ppermute | solution.py:362
  49.7 0.1 collective-permute-start.13
  49.8 2.7 %collective-permute-done.7 = f32[512,128]{1,0:T(8,128)S(1)} collective-permute-done((f32[512,128]{1,0:T(8,128)S(1)}, f32[512,128]{1,0:T(8,128)S(1)}, u32[]{:S(2)}, u32[]{:S(2)}) %collective-permute-start.7) | collective-permute-done | bytes 262176 | tf_op jit(solution)/shard_map/ppermute | solution.py:400
  52.5 1.0 %collective-permute-done.13 = f32[32,128]{1,0:T(8,128)S(1)} collective-permute-done((f32[32,128]{1,0:T(8,128)S(1)}, f32[32,128]{1,0:T(8,128)S(1)}, u32[]{:S(2)}, u32[]{:S(2)}) %collective-permute-start.13) | collective-permute-done | bytes 16416 | tf_op jit(solution)/shard_map/ppermute | solution.py:353
  53.5 0.6 %slice_add_fusion = f32[32,128]{1,0:T(8,128)} fusion(f32[32,128]{1,0:T(8,128)S(1)} %collective-permute-done.13, f32[64,128]{1,0:T(8,128)S(1)} %add_add_fusion), kind=kLoop, calls=%fused_computation.4 | loop fusion | flops 4096 | bytes 49152 | tf_op jit(solution)/shard_map/add | solution.py:410
  54.1 0.9 %maximum_add_fusion = f32[1024,128]{1,0:T(8,128)} fusion(f32[1024,128]{1,0:T(8,128)S(1)} %get-tuple-element.54, f32[512,128]{1,0:T(8,128)S(1)} %collective-permute-done.8, f32[512,128]{1,0:T(8,128)S(1)} %collective-permute-done.7), kind=kLoop, calls=%fused_computation | loop fusion | flops 262144 | bytes 1572864 | tf_op jit(solution)/shard_map/add | solution.py:409
  (10 shorter events, 0.1 us)
Async XLA Ops:
  0.6 11.0 %collective-permute-start.2 = (f32[32,128]{1,0:T(8,128)}, f32[32,128]{1,0:T(8,128)S(1)}, u32[]{:S(2)}, u32[]{:S(2)}) collective-permute-start(f32[32,128]{1,0:T(8,128)} %bitcast.23), channel_id=1, source_target_pairs={{0,12},{1,13},{2,14},{3,15},{4,8},{5,9},{6,10},{7,11},{8,4},{9,5},... | collective-permute-start | bytes 49160 | tf_op jit(solution)/shard_map/ppermute | solution.py:353
  5.7 5.9 %collective-permute-start.1 = (f32[32,128]{1,0:T(8,128)}, f32[32,128]{1,0:T(8,128)S(1)}, u32[]{:S(2)}, u32[]{:S(2)}) collective-permute-start(f32[32,128]{1,0:T(8,128)} %bitcast.24), channel_id=1, source_target_pairs={{0,4},{1,5},{2,6},{3,7},{4,0},{5,1},{6,2},{7,3},{8,12},{9,13},{10,... | collective-permute-start | bytes 49160 | tf_op jit(solution)/shard_map/ppermute | solution.py:353
  5.7 5.9 %collective-permute-start = (f32[32,128]{1,0:T(8,128)}, f32[32,128]{1,0:T(8,128)S(1)}, u32[]{:S(2)}, u32[]{:S(2)}) collective-permute-start(f32[32,128]{1,0:T(8,128)} %bitcast.25), channel_id=1, source_target_pairs={{0,8},{1,9},{2,10},{3,11},{4,12},{5,13},{6,14},{7,15},{8,0},{9,1},... | collective-permute-start | bytes 49160 | tf_op jit(solution)/shard_map/ppermute | solution.py:353
  6.4 5.2 %copy-start.3 = (f32[8,2,2,128]{3,2,1,0:T(2,128)S(1)}, f32[8,2,2,128]{3,2,1,0:T(2,128)}, u32[]{:S(2)}) copy-start(f32[8,2,2,128]{3,2,1,0:T(2,128)} %param.8) | copy-start | bytes 49156
  6.4 8.7 %copy-start = (f32[128,2,2,256]{3,2,1,0:T(2,128)S(1)}, f32[128,2,2,256]{3,2,1,0:T(2,128)}, u32[]{:S(2)}) copy-start(f32[128,2,2,256]{3,2,1,0:T(2,128)} %param.7) | copy-start | bytes 1572868
  7.6 14.0 %collective-permute-start.5 = (f32[512,128]{1,0:T(8,128)S(1)}, f32[512,128]{1,0:T(8,128)S(1)}, u32[]{:S(2)}, u32[]{:S(2)}) collective-permute-start(f32[512,128]{1,0:T(8,128)S(1)} %bitcast.21), channel_id=1, source_target_pairs={{1,0},{2,1},{3,2},{4,3},{5,4},{6,5},{7,6},{8,7},{9,8},{10,9},{11,1... | collective-permute-start | bytes 786440 | tf_op jit(solution)/shard_map/ppermute | solution.py:383
  11.7 0.7 %copy-start.4 = (s32[16]{0:T(128)S(1)}, s32[16]{0:T(128)}, u32[]{:S(2)}) copy-start(s32[16]{0:T(128)} %param.10) | copy-start | bytes 196
  13.1 4.9 %collective-permute-start.3 = (f32[128,128]{1,0:T(8,128)S(1)}, f32[128,128]{1,0:T(8,128)S(1)}, u32[]{:S(2)}, u32[]{:S(2)}) collective-permute-start(f32[128,128]{1,0:T(8,128)S(1)} %pad_maximum_fusion.1), channel_id=1, source_target_pairs={{0,2},{1,3},{2,0},{3,1},{4,6},{5,7},{6,4},{7,5},{8,10},{9,11},{10,... | collective-permute-start | bytes 196616 | tf_op jit(solution)/shard_map/ppermute | solution.py:353
  13.7 0.7 %copy-start.5 = (s32[16]{0:T(128)S(1)}, s32[16]{0:T(128)}, u32[]{:S(2)}) copy-start(s32[16]{0:T(128)} %param.11) | copy-start | bytes 196
  15.1 1.2 %copy-start.1 = (f32[16,128,128]{2,1,0:T(8,128)S(1)}, f32[16,128,128]{2,1,0:T(8,128)}, u32[]{:S(2)}) copy-start(f32[16,128,128]{2,1,0:T(8,128)} %patterns_ref) | copy-start | bytes 3145732
  16.4 1.1 %copy-start.2 = (f32[12,128,128]{2,1,0:T(8,128)S(1)}, f32[12,128,128]{2,1,0:T(8,128)}, u32[]{:S(2)}) copy-start(f32[12,128,128]{2,1,0:T(8,128)} %constant.10.clone.factors_ref) | copy-start | bytes 2359300
  18.1 3.5 %collective-permute-start.6 = (f32[256,128]{1,0:T(8,128)S(1)}, f32[256,128]{1,0:T(8,128)S(1)}, u32[]{:S(2)}, u32[]{:S(2)}) collective-permute-start(f32[256,128]{1,0:T(8,128)S(1)} %pad_maximum_fusion.refs_2_), channel_id=1, source_target_pairs={{0,1},{1,0},{2,3},{3,2},{4,5},{5,4},{6,7},{7,6},{8,9},{9,8},{10,11... | collective-permute-start | bytes 393224 | tf_op jit(solution)/shard_map/ppermute | solution.py:353
  18.2 7.3 %collective-permute-start.4 = (f32[512,128]{1,0:T(8,128)S(1)}, f32[512,128]{1,0:T(8,128)S(1)}, u32[]{:S(2)}, u32[]{:S(2)}) collective-permute-start(f32[512,128]{1,0:T(8,128)S(1)} %bitcast.20), channel_id=1, source_target_pairs={{1,0},{2,1},{3,2},{4,3},{5,4},{6,5},{7,6},{8,7},{9,8},{10,9},{11,1... | collective-permute-start | bytes 786440 | tf_op jit(solution)/shard_map/ppermute | solution.py:392
  30.7 8.7 %collective-permute-start.8 = (f32[512,128]{1,0:T(8,128)S(1)}, f32[512,128]{1,0:T(8,128)S(1)}, u32[]{:S(2)}, u32[]{:S(2)}) collective-permute-start(f32[512,128]{1,0:T(8,128)S(1)} %get-tuple-element.56), channel_id=1, source_target_pairs={{0,1},{1,2},{2,3},{3,4},{4,5},{5,6},{6,7},{7,8},{8,9},{9,10},{10,1... | collective-permute-start | bytes 786440 | tf_op jit(solution)/shard_map/ppermute | solution.py:397
  33.3 1.4 %collective-permute-start.9 = (f32[256,128]{1,0:T(8,128)S(1)}, f32[256,128]{1,0:T(8,128)S(1)}, u32[]{:S(2)}, u32[]{:S(2)}) collective-permute-start(f32[256,128]{1,0:T(8,128)S(1)} %get-tuple-element.59), channel_id=1, source_target_pairs={{0,1},{1,0},{2,3},{3,2},{4,5},{5,4},{6,7},{7,6},{8,9},{9,8},{10,11... | collective-permute-start | bytes 393224 | tf_op jit(solution)/shard_map/ppermute | solution.py:353
  39.4 4.9 %collective-permute-start.11 = (f32[64,128]{1,0:T(8,128)S(1)}, f32[64,128]{1,0:T(8,128)S(1)}, u32[]{:S(2)}, u32[]{:S(2)}) collective-permute-start(f32[64,128]{1,0:T(8,128)S(1)} %get-tuple-element.66), channel_id=1, source_target_pairs={{0,8},{1,9},{2,10},{3,11},{4,12},{5,13},{6,14},{7,15},{8,0},{9,1},... | collective-permute-start | bytes 98312 | tf_op jit(solution)/shard_map/ppermute | solution.py:362
  41.3 4.3 %collective-permute-start.12 = (f32[64,128]{1,0:T(8,128)S(1)}, f32[64,128]{1,0:T(8,128)S(1)}, u32[]{:S(2)}, u32[]{:S(2)}) collective-permute-start(f32[64,128]{1,0:T(8,128)S(1)} %get-tuple-element.67), channel_id=1, source_target_pairs={{0,12},{1,13},{2,14},{3,15},{4,0},{5,1},{6,2},{7,3},{8,4},{9,5},{1... | collective-permute-start | bytes 98312 | tf_op jit(solution)/shard_map/ppermute | solution.py:362
  44.0 5.7 %collective-permute-start.10 = (f32[64,128]{1,0:T(8,128)S(1)}, f32[64,128]{1,0:T(8,128)S(1)}, u32[]{:S(2)}, u32[]{:S(2)}) collective-permute-start(f32[64,128]{1,0:T(8,128)S(1)} %get-tuple-element.68), channel_id=1, source_target_pairs={{0,4},{1,5},{2,6},{3,7},{4,8},{5,9},{6,10},{7,11},{8,12},{9,13},{1... | collective-permute-start | bytes 98312 | tf_op jit(solution)/shard_map/ppermute | solution.py:362
  44.0 8.5 %collective-permute-start.7 = (f32[512,128]{1,0:T(8,128)S(1)}, f32[512,128]{1,0:T(8,128)S(1)}, u32[]{:S(2)}, u32[]{:S(2)}) collective-permute-start(f32[512,128]{1,0:T(8,128)S(1)} %get-tuple-element.55), channel_id=1, source_target_pairs={{0,1},{1,2},{2,3},{3,4},{4,5},{5,6},{6,7},{7,8},{8,9},{9,10},{10,1... | collective-permute-start | bytes 786440 | tf_op jit(solution)/shard_map/ppermute | solution.py:400
  49.7 3.8 %collective-permute-start.13 = (f32[32,128]{1,0:T(8,128)S(1)}, f32[32,128]{1,0:T(8,128)S(1)}, u32[]{:S(2)}, u32[]{:S(2)}) collective-permute-start(f32[32,128]{1,0:T(8,128)S(1)} %slice.26), channel_id=1, source_target_pairs={{0,2},{1,3},{2,0},{3,1},{4,6},{5,7},{6,4},{7,5},{8,10},{9,11},{10,... | collective-permute-start | bytes 49160 | tf_op jit(solution)/shard_map/ppermute | solution.py:353
